TPU v7x, 32 devices: a whole 2x2x4 slice. The times are simulated.
32 devices in a mesh: groups: 2 (over x), sec: 16 (over z, y, core).
Axes of the slice: x: 2, y: 2, z: 4, core: 2. Of those that a mesh axis runs over, the one named last changes fastest.
Arguments:
- two_site: bfloat16 [64, 256, 256], P(('groups', 'sec')), parts along dimension 0, may hold values from -6 to 6
- left_size: int32 [64], P(('groups', 'sec')), parts along dimension 0, may hold values from 64 to 256, as said below
- right_size: int32 [64], P(('groups', 'sec')), parts along dimension 0, may hold values from 64 to 256, as said below
- term_shift: int32 [48], P('groups'), parts along dimension 0, may hold values from -1 to 1
- route_offset: int32 [96], P('groups'), parts along dimension 0, may hold values from 0 to 15, as said below
- left_env: bfloat16 [64, 24, 256, 256], P(('groups', 'sec')), parts along dimension 0, may hold values from -0.375 to 0.375
- right_env: bfloat16 [1536, 256, 256], P(('groups', 'sec')), parts along dimension 0, may hold values from -0.078125 to 0.078125
Outputs:
- hamiltonian_theta: bfloat16 [64, 256, 256], P(('groups', 'sec')), parts along dimension 0
There are 2 independent parts, one for each index of `groups`. A program takes and returns all parts, laid end to end along the dimension named above; each array names one. Nothing has to cross between parts.
Inputs may be any that keep to these rules, and one draw needn't show every extreme that they name: `left_size`: some sector has 256 live left states. `right_size`: some sector has 256 live right states. `route_offset`: each value appears at most 3 times and some value exactly 3 times.
All inputs are finite; a program needn't handle non-finite values.
Results may differ from a plain program's by a relative error of at most 0.01.
Values may be sent and summed in bfloat16 or wider, within the bound.
A program may use at most 128 MiB of HBM per device.

v0:
```python
import jax
import jax.numpy as jnp
from jax import lax
from jax.sharding import PartitionSpec as P


def padded_2(block, sides, width):
    for axis, dim in sides:
        count = lax.axis_size(axis)
        forward = [(i, i + 1) for i in range(count - 1)]
        backward = [(target, source) for source, target in forward]
        low = lax.ppermute(
            lax.slice_in_dim(block, block.shape[dim] - width, None, axis=dim), axis, forward
        )
        high = lax.ppermute(lax.slice_in_dim(block, 0, width, axis=dim), axis, backward)
        block = jnp.concatenate([low, block, high], axis=dim)
    return block


def live_region(left_size, right_size, states):
    positions = jnp.arange(states, dtype=jnp.int32)
    return (positions[None, :, None] < left_size[:, None, None]) & (
        positions[None, None, :] < right_size[:, None, None]
    )


def arrange(blocks, positions, slot_total):
    unit_total = blocks.shape[0]
    matches = (positions[None, :] == jnp.arange(slot_total, dtype=jnp.int32)[:, None]).astype(
        jnp.int32
    )
    picked = jnp.sum(matches * jnp.arange(unit_total, dtype=jnp.int32)[None, :], axis=1)
    picked = picked + unit_total * (1 - jnp.sum(matches, axis=1))
    return jnp.take(blocks, picked, axis=0, mode="fill", fill_value=0)


def local(two_site, left_size, right_size, term_shift, route_offset, left_env, right_env):
    members = lax.axis_size("sec")
    own_index = lax.axis_index("sec")
    sec_local = two_site.shape[0]
    states = two_site.shape[1]
    term_count = left_env.shape[1]
    unit_count = sec_local * term_count
    slot_count = (unit_count + members - 1) // members
    slot_total = members * slot_count
    live_mask = live_region(left_size, right_size, states)
    masked = jnp.where(live_mask, two_site, jnp.zeros_like(two_site))
    padded = padded_2(masked, (("sec", 0),), 1)
    unit_index = jnp.arange(unit_count, dtype=jnp.int32)
    source_index = unit_index // term_count + 1 - jnp.tile(term_shift, sec_local)
    sources = jnp.take(padded, source_index, axis=0)
    left_blocks = left_env.reshape(unit_count, states, states)
    projected = jnp.einsum(
        "uab,ubc->uac", left_blocks, sources, preferred_element_type=jnp.float32
    ).astype(jnp.bfloat16)
    same_offset = route_offset[None, :] == route_offset[:, None]
    earlier = unit_index[None, :] < unit_index[:, None]
    unit_rank = jnp.sum((same_offset & earlier).astype(jnp.int32), axis=1)
    send_slot = jnp.mod(own_index + route_offset, members) * slot_count + unit_rank
    receive_slot = jnp.mod(own_index - route_offset, members) * slot_count + unit_rank
    outgoing = arrange(projected, send_slot, slot_total)
    arrived = lax.all_to_all(outgoing, "sec", split_axis=0, concat_axis=0, tiled=True)
    incoming = jnp.take(arrived, receive_slot, axis=0)
    partial_value = jnp.einsum(
        "uab,ucb->uac", incoming, right_env, preferred_element_type=jnp.float32
    ).astype(jnp.bfloat16)
    returned = lax.all_to_all(
        arrange(partial_value, receive_slot, slot_total),
        "sec",
        split_axis=0,
        concat_axis=0,
        tiled=True,
    )
    term_result = jnp.take(returned, send_slot, axis=0)
    summed = jnp.sum(
        term_result.reshape(sec_local, term_count, states, states), axis=1, dtype=jnp.float32
    )
    return jnp.where(live_mask, summed, jnp.zeros_like(summed)).astype(jnp.bfloat16)


def solution(mesh):
    in_specs = (
        P(("groups", "sec"), None, None),
        P(("groups", "sec")),
        P(("groups", "sec")),
        P("groups"),
        P("groups"),
        P(("groups", "sec"), None, None, None),
        P(("groups", "sec"), None, None),
    )
    out_specs = P(("groups", "sec"), None, None)
    return jax.shard_map(local, mesh=mesh, in_specs=in_specs, out_specs=out_specs, check_vma=False)
```

profile of v0, /device:TPU:18, one launch (start us, length us, event | category | flops | bytes accessed | tf_op | source)
XLA Modules:
  0.0 380.6 jit_solution(8290029440839997554)
XLA Ops:
  0.0 0.7 iota_compare_fusion.3
  0.7 1.1 and_select_fusion.1
  1.9 1.9 collective-permute-start
  3.8 4.5 %collective-permute-start.1 = (bf16[1,256,256]{2,1,0:T(8,128)(2,1)S(1)}, bf16[1,256,256]{2,1,0:T(8,128)(2,1)S(1)}, u32[]{:S(2)}, u32[]{:S(2)}) collective-permute-start(bf16[1,256,256]{2,1,0:T(8,128)(2,1)S(1)} %get-tuple-element.20), channel_id=1, source_target_pairs={{1,0},{2,1},{3,2},{4,3},{5,4},{6,5},{7,6},{8,7},{9,8},{10,9},{11,1... | collective-permute-start | bytes 393224 | tf_op jit(solution)/shard_map/ppermute | solution.py:15
  8.4 0.7 tile.11
  9.0 0.1 tile.13
  9.1 0.1 tile.12
  9.2 0.9 convert_reduce_fusion.3
  10.1 0.7 compare_and_fusion.2
  10.8 0.1 convert_reduce_fusion.1
  11.0 0.0 collective-permute-done
  11.0 0.0 collective-permute-done.1
  11.0 0.1 pad_maximum_fusion
  11.1 4.9 %gather_fusion = bf16[48,256,256]{2,1,0:T(8,128)(2,1)} fusion(bf16[4,256,256]{2,1,0:T(8,128)(2,1)S(1)} %pad_maximum_fusion, s32[1024]{0:T(1024)S(1)} %pad_clamp_fusion.4), kind=kCustom, calls=%fused_computation.4 | custom fusion | bytes 12583104 | tf_op jit(solution)/shard_map/jit(_take)/gather | solution.py:51
  16.0 12.6 %convert_bitcast_fusion = bf16[48,256,256]{1,2,0:T(8,128)(2,1)} fusion(bf16[48,256,256]{2,1,0:T(8,128)(2,1)} %bitcast.10, bf16[48,256,256]{2,1,0:T(8,128)(2,1)} %gather_fusion, pred[48]{0:T(512)(128)(4,1)S(1)} %compare_and_fusion.4), kind=kOutput, calls=%fused_computation.8 | convolution fusion | flops 1616904192 | bytes 18874416 | tf_op jit(solution)/shard_map/uab,ubc->uac/dot_general | solution.py:53
  28.6 8.6 %copy.9 = bf16[48,256,256]{2,1,0:T(8,128)(2,1)} copy(bf16[48,256,256]{1,2,0:T(8,128)(2,1)} %convert_bitcast_fusion) | data formatting | bytes 12582912 | tf_op jit(solution)/shard_map/convert_element_type | solution.py:55
  37.2 7.8 %gather_fusion.1 = bf16[48,256,256]{2,1,0:T(8,128)(2,1)} fusion(bf16[48,256,256]{2,1,0:T(8,128)(2,1)} %copy.9, s32[1024]{0:T(1024)S(1)} %pad_clamp_fusion.3), kind=kCustom, calls=%fused_computation.clone | custom fusion | bytes 12583104 | tf_op jit(solution)/shard_map/jit(_take)/gather | solution.py:34
  45.0 5.9 %broadcast_select_fusion.2 = bf16[48,256,256]{2,1,0:T(8,128)(2,1)} fusion(bf16[48,256,256]{2,1,0:T(8,128)(2,1)} %gather_fusion.1, pred[48]{0:T(512)(128)(4,1)S(1)} %get-tuple-element.17), kind=kLoop, calls=%fused_computation.14 | loop fusion | flops 3145728 | bytes 12582960 | tf_op jit(solution)/shard_map/jit(_take)/select_n | solution.py:34
  50.9 6.3 %all-to-all-start = ((bf16[48,256,256]{2,1,0:T(8,128)(2,1)}), bf16[48,256,256]{2,1,0:T(8,128)(2,1)}, u32[]{:S(2)}, u32[]{:S(2)}) async-start(bf16[48,256,256]{2,1,0:T(8,128)(2,1)} %broadcast_select_fusion.2), calls=%async_computation | async-start | bytes 12582912 | tf_op jit(solution)/shard_map/all_to_all | solution.py:62
  57.3 137.6 %all-to-all-done = bf16[48,256,256]{2,1,0:T(8,128)(2,1)} async-done(((bf16[48,256,256]{2,1,0:T(8,128)(2,1)}), bf16[48,256,256]{2,1,0:T(8,128)(2,1)}, u32[]{:S(2)}, u32[]{:S(2)}) %all-to-all-start) | async-done | bytes 6291488 | tf_op jit(solution)/shard_map/all_to_all | solution.py:62
  194.9 7.8 %gather_fusion.2 = bf16[48,256,256]{2,1,0:T(8,128)(2,1)} fusion(bf16[48,256,256]{2,1,0:T(8,128)(2,1)} %all-to-all-done, s32[1024]{0:T(1024)S(1)} %pad_clamp_fusion.2), kind=kCustom, calls=%fused_computation.1.clone | custom fusion | bytes 12583104 | tf_op jit(solution)/shard_map/jit(_take)/gather | solution.py:63
  202.6 9.1 %fusion.8 = bf16[48,256,256]{2,1,0:T(8,128)(2,1)} fusion(bf16[48,256,256]{2,1,0:T(8,128)(2,1)} %param.17, bf16[48,256,256]{2,1,0:T(8,128)(2,1)} %gather_fusion.2, pred[48]{0:T(512)(128)(4,1)S(1)} %get-tuple-element.15), kind=kOutput, calls=%fused_computation.16 | convolution fusion | flops 1616904192 | bytes 18874416 | tf_op jit(solution)/shard_map/uab,ucb->uac/dot_general | solution.py:64
  211.8 7.8 %gather_fusion.3 = bf16[48,256,256]{2,1,0:T(8,128)(2,1)} fusion(bf16[48,256,256]{2,1,0:T(8,128)(2,1)} %fusion.8, s32[1024]{0:T(1024)S(1)} %pad_clamp_fusion.1), kind=kCustom, calls=%fused_computation.2.clone | custom fusion | bytes 12583104 | tf_op jit(solution)/shard_map/jit(_take)/gather | solution.py:34
  219.5 5.9 %broadcast_select_fusion.1 = bf16[48,256,256]{2,1,0:T(8,128)(2,1)} fusion(bf16[48,256,256]{2,1,0:T(8,128)(2,1)} %gather_fusion.3, pred[48]{0:T(512)(128)(4,1)S(1)} %get-tuple-element.13), kind=kLoop, calls=%fused_computation.12 | loop fusion | flops 3145728 | bytes 12582960 | tf_op jit(solution)/shard_map/jit(_take)/select_n | solution.py:34
  225.4 4.7 %all-to-all-start.1 = ((bf16[48,256,256]{2,1,0:T(8,128)(2,1)}), bf16[48,256,256]{2,1,0:T(8,128)(2,1)}, u32[]{:S(2)}, u32[]{:S(2)}) async-start(bf16[48,256,256]{2,1,0:T(8,128)(2,1)} %broadcast_select_fusion.1), calls=%async_computation.1 | async-start | bytes 12582912 | tf_op jit(solution)/shard_map/all_to_all | solution.py:67
  230.2 137.6 %all-to-all-done.1 = bf16[48,256,256]{2,1,0:T(8,128)(2,1)} async-done(((bf16[48,256,256]{2,1,0:T(8,128)(2,1)}), bf16[48,256,256]{2,1,0:T(8,128)(2,1)}, u32[]{:S(2)}, u32[]{:S(2)}) %all-to-all-start.1) | async-done | bytes 6291488 | tf_op jit(solution)/shard_map/all_to_all | solution.py:67
  367.8 7.7 %gather_fusion.4 = bf16[48,256,256]{2,1,0:T(8,128)(2,1)} fusion(bf16[48,256,256]{2,1,0:T(8,128)(2,1)} %all-to-all-done.1, s32[1024]{0:T(1024)S(1)} %pad_clamp_fusion), kind=kCustom, calls=%fused_computation.3.clone | custom fusion | bytes 12583104 | tf_op jit(solution)/shard_map/jit(_take)/gather | solution.py:74
  375.5 3.4 broadcast_select_fusion
  379.0 0.8 convert_reduce_fusion
  379.8 0.8 fusion.13
  (12 shorter events, 0.1 us)
Async XLA Ops:
  1.9 9.1 %collective-permute-start = (bf16[1,256,256]{2,1,0:T(8,128)(2,1)S(1)}, bf16[1,256,256]{2,1,0:T(8,128)(2,1)S(1)}, u32[]{:S(2)}, u32[]{:S(2)}) collective-permute-start(bf16[1,256,256]{2,1,0:T(8,128)(2,1)S(1)} %get-tuple-element.19), channel_id=1, source_target_pairs={{0,1},{1,2},{2,3},{3,4},{4,5},{5,6},{6,7},{7,8},{8,9},{9,10},{10,1... | collective-permute-start | bytes 393224 | tf_op jit(solution)/shard_map/ppermute | solution.py:12
  3.8 7.2 %collective-permute-start.1 = (bf16[1,256,256]{2,1,0:T(8,128)(2,1)S(1)}, bf16[1,256,256]{2,1,0:T(8,128)(2,1)S(1)}, u32[]{:S(2)}, u32[]{:S(2)}) collective-permute-start(bf16[1,256,256]{2,1,0:T(8,128)(2,1)S(1)} %get-tuple-element.20), channel_id=1, source_target_pairs={{1,0},{2,1},{3,2},{4,3},{5,4},{6,5},{7,6},{8,7},{9,8},{10,9},{11,1... | collective-permute-start | bytes 393224 | tf_op jit(solution)/shard_map/ppermute | solution.py:15
  50.9 144.0 %all-to-all-start = ((bf16[48,256,256]{2,1,0:T(8,128)(2,1)}), bf16[48,256,256]{2,1,0:T(8,128)(2,1)}, u32[]{:S(2)}, u32[]{:S(2)}) async-start(bf16[48,256,256]{2,1,0:T(8,128)(2,1)} %broadcast_select_fusion.2), calls=%async_computation | async-start | bytes 12582912 | tf_op jit(solution)/shard_map/all_to_all | solution.py:62
  225.4 142.3 %all-to-all-start.1 = ((bf16[48,256,256]{2,1,0:T(8,128)(2,1)}), bf16[48,256,256]{2,1,0:T(8,128)(2,1)}, u32[]{:S(2)}, u32[]{:S(2)}) async-start(bf16[48,256,256]{2,1,0:T(8,128)(2,1)} %broadcast_select_fusion.1), calls=%async_computation.1 | async-start | bytes 12582912 | tf_op jit(solution)/shard_map/all_to_all | solution.py:67
where the time goes:
time: 382 us; the launch traced here: 381 us
  waiting for transfers between devices  275 us (72%)
  local copies, waits for them, and re-layouts  45.4 us (12%)
  matrix products  21.7 us (6%)
  other arithmetic  20.7 us (5%)
  starting transfers between devices  17.5 us (5%)
    all_to_all x1, waiting for transfers between devices, local(): lax.all_to_all(outgoing, 'sec', split_axis=0, concat_axis=0, tiled=True)  138 us
    all_to_all x1, waiting for transfers between devices, local(): lax.all_to_all(arrange(partial_value, receive_slot, slot_total), 'sec', s...  138 us
    gather x2, local copies, waits for them, and re-layouts, arrange(): return jnp.take(blocks, picked, axis=0, mode='fill', fill_value=0)  15.5 us
    dot_general x1, matrix products, local(): jnp.einsum('uab,ubc->uac', left_blocks, sources, preferred_element_type=j...  12.6 us
    select_n x2, other arithmetic, arrange(): return jnp.take(blocks, picked, axis=0, mode='fill', fill_value=0)  11.8 us
    dot_general x1, matrix products, local(): jnp.einsum('uab,ucb->uac', incoming, right_env, preferred_element_type=jn...  9.12 us
    convert_element_type x1, local copies, waits for them, and re-layouts, local(): projected = jnp.einsum('uab,ubc->uac', left_blocks, sources, preferred_el...  8.62 us
    gather x1, local copies, waits for them, and re-layouts, local(): incoming = jnp.take(arrived, receive_slot, axis=0)  7.76 us
  transfers between devices with their start and end apart: 4, of which 2 were waited for; matrix products, arithmetic and copies ran while one was open for 1% of the time, Pallas kernels for 0%

commit v1 on v0

v1 whole, which is shorter than its diff:
```python
import functools

import jax
import jax.numpy as jnp
from jax import lax
from jax.experimental import pallas as pl
from jax.experimental.pallas import tpu as pltpu
from jax.sharding import PartitionSpec as P


def live_region(rows, columns, states):
    row = lax.broadcasted_iota(jnp.int32, (states, states), 0)
    column = lax.broadcasted_iota(jnp.int32, (states, states), 1)
    return (row < rows) & (column < columns)


def kernel(
    members,
    slots,
    picked_ref,
    shift_ref,
    left_size_ref,
    right_size_ref,
    two_site_ref,
    left_env_ref,
    right_env_ref,
    out_ref,
    left_vmem,
    right_vmem,
    outgoing,
    incoming,
    projected,
    padded,
    total,
    left_sem,
    right_sem,
    edge_send_sem,
    edge_recv_sem,
    send_sem,
    recv_sem,
):
    own = lax.axis_index("sec")
    sec_local, states = two_site_ref.shape[0], two_site_ref.shape[1]
    unit_count = left_env_ref.shape[0]
    term_count = unit_count // sec_local

    right_copy = pltpu.make_async_copy(right_env_ref, right_vmem, right_sem)
    right_copy.start()
    left_copy = pltpu.make_async_copy(left_env_ref, left_vmem, left_sem)
    left_copy.start()

    barrier = pltpu.get_barrier_semaphore()

    def greet(step, carry):
        peer = lax.rem(own + step, members)
        pl.semaphore_signal(barrier, inc=1, device_id={"sec": peer})
        return carry

    lax.fori_loop(1, members, greet, 0)

    for sector in range(sec_local):
        live = live_region(left_size_ref[sector], right_size_ref[sector], states)
        block = two_site_ref[sector]
        padded[1 + sector] = jnp.where(live, block, jnp.zeros_like(block))

    pl.semaphore_wait(barrier, members - 1)

    def edge_copy(source, target, index, peer):
        return pltpu.make_async_remote_copy(
            src_ref=padded.at[source],
            dst_ref=padded.at[target],
            send_sem=edge_send_sem.at[index],
            recv_sem=edge_recv_sem.at[index],
            device_id={"sec": peer},
        )

    up = edge_copy(sec_local, 0, 0, lax.rem(own + 1, members))
    down = edge_copy(1, sec_local + 1, 1, lax.rem(own + members - 1, members))
    has_up, has_down = own < members - 1, own > 0

    pl.when(has_up)(up.start)
    pl.when(has_down)(down.start)

    def block_copy(offset, peer):
        return pltpu.make_async_remote_copy(
            src_ref=outgoing.at[pl.ds(offset * slots, slots)],
            dst_ref=incoming.at[pl.ds(offset * slots, slots)],
            send_sem=send_sem.at[offset],
            recv_sem=recv_sem.at[offset],
            device_id={"sec": peer},
        )

    right_copy.wait()

    def order(step):
        return lax.rem(members // 2 + step, members)

    def send(step, carry):
        offset = order(step)

        @pl.when(offset > 0)
        def _():
            for slot in range(slots):
                unit = jnp.minimum(picked_ref[offset * slots + slot], unit_count - 1)
                outgoing[offset * slots + slot] = right_vmem[unit]
            block_copy(offset, lax.rem(own - offset + members, members)).start()

        @pl.when(offset == 0)
        def _():
            for slot in range(slots):
                unit = jnp.minimum(picked_ref[slot], unit_count - 1)
                incoming[slot] = right_vmem[unit]

        return carry

    lax.fori_loop(0, members, send, 0)

    @pl.when(own == 0)
    def _():
        padded[0] = jnp.zeros_like(padded[0])

    @pl.when(own == members - 1)
    def _():
        padded[sec_local + 1] = jnp.zeros_like(padded[0])

    pl.when(has_up)(up.wait_send)
    pl.when(has_down)(down.wait_send)
    pl.when(has_down)(up.wait_recv)
    pl.when(has_up)(down.wait_recv)
    left_copy.wait()

    def project(unit, carry):
        source = padded[unit // term_count + 1 - shift_ref[unit % term_count]]
        projected[unit] = jnp.dot(
            left_vmem[unit], source, preferred_element_type=jnp.float32
        ).astype(jnp.bfloat16)
        return carry

    lax.fori_loop(0, unit_count, project, 0)

    total[...] = jnp.zeros_like(total)

    def multiply(offset):
        for slot in range(slots):
            unit = picked_ref[offset * slots + slot]
            factor = projected[jnp.minimum(unit, unit_count - 1)]
            value = lax.dot_general(
                factor,
                incoming[offset * slots + slot],
                (((1,), (1,)), ((), ())),
                preferred_element_type=jnp.float32,
            )
            for sector in range(sec_local):
                mine = unit // term_count == sector
                total[sector] += jnp.where(mine, value, jnp.zeros_like(value))

    multiply(0)

    def arrive(step, carry):
        half = step // 2
        offset = jnp.where(step % 2 == 0, half + 1, members - 1 - half)
        block_copy(offset, lax.rem(own - offset + members, members)).wait_recv()
        multiply(offset)
        return carry

    lax.fori_loop(0, members - 1, arrive, 0)

    def sent(offset, carry):
        block_copy(offset, lax.rem(own - offset + members, members)).wait_send()
        return carry

    lax.fori_loop(1, members, sent, 0)

    for sector in range(sec_local):
        live = live_region(left_size_ref[sector], right_size_ref[sector], states)
        value = total[sector]
        out_ref[sector] = jnp.where(live, value, jnp.zeros_like(value)).astype(out_ref.dtype)


def local(two_site, left_size, right_size, term_shift, route_offset, left_env, right_env):
    members = lax.axis_size("sec")
    sec_local, states = two_site.shape[0], two_site.shape[1]
    unit_count = right_env.shape[0]
    slots = (unit_count + members - 1) // members
    slot_total = members * slots
    unit_index = jnp.arange(unit_count, dtype=jnp.int32)
    same_offset = route_offset[None, :] == route_offset[:, None]
    earlier = unit_index[None, :] < unit_index[:, None]
    unit_rank = jnp.sum((same_offset & earlier).astype(jnp.int32), axis=1)
    place = route_offset * slots + unit_rank
    slot_index = jnp.arange(slot_total, dtype=jnp.int32)
    picked = unit_count + jnp.sum(
        jnp.where(place[None, :] == slot_index[:, None], unit_index[None, :] - unit_count, 0),
        axis=1,
    )
    block = (states, states)
    smem = pl.BlockSpec(memory_space=pltpu.SMEM)
    vmem = pl.BlockSpec(memory_space=pltpu.VMEM)
    hbm = pl.BlockSpec(memory_space=pl.ANY)
    return pl.pallas_call(
        functools.partial(kernel, members, slots),
        out_shape=jax.ShapeDtypeStruct(two_site.shape, two_site.dtype),
        in_specs=[smem, smem, smem, smem, vmem, hbm, hbm],
        out_specs=vmem,
        scratch_shapes=[
            pltpu.VMEM((unit_count,) + block, jnp.bfloat16),
            pltpu.VMEM((unit_count,) + block, jnp.bfloat16),
            pltpu.VMEM((slot_total,) + block, jnp.bfloat16),
            pltpu.VMEM((slot_total,) + block, jnp.bfloat16),
            pltpu.VMEM((unit_count,) + block, jnp.bfloat16),
            pltpu.VMEM((sec_local + 2,) + block, jnp.bfloat16),
            pltpu.VMEM((sec_local,) + block, jnp.float32),
            pltpu.SemaphoreType.DMA,
            pltpu.SemaphoreType.DMA,
            pltpu.SemaphoreType.DMA((2,)),
            pltpu.SemaphoreType.DMA((2,)),
            pltpu.SemaphoreType.DMA((members,)),
            pltpu.SemaphoreType.DMA((members,)),
        ],
        compiler_params=pltpu.CompilerParams(
            collective_id=0, has_side_effects=True, vmem_limit_bytes=50 * 1024 * 1024
        ),
        name="route_and_multiply",
    )(
        picked,
        term_shift,
        left_size,
        right_size,
        two_site,
        left_env.reshape((unit_count,) + block),
        right_env,
    )


def solution(mesh):
    in_specs = (
        P(("groups", "sec"), None, None),
        P(("groups", "sec")),
        P(("groups", "sec")),
        P("groups"),
        P("groups"),
        P(("groups", "sec"), None, None, None),
        P(("groups", "sec"), None, None),
    )
    out_specs = P(("groups", "sec"), None, None)
    return jax.shard_map(local, mesh=mesh, in_specs=in_specs, out_specs=out_specs, check_vma=False)
```

time: 382 us -> 152 us (0.40)
  waiting for transfers between devices: 275 us -> 0 us
  Pallas kernels: 0 us -> 147 us
  local copies, waits for them, and re-layouts: 45.4 us -> 3.62 us
  matrix products: 21.7 us -> 0 us
  other arithmetic: 20.7 us -> 1.69 us
  starting transfers between devices: 17.5 us -> 0 us
    all_to_all x2 -> x0, waiting for transfers between devices: 275 us -> none  [the longest x1 138 us: local(): lax.all_to_all(outgoing, 'sec', split_axis=0, concat_axis=0, tiled=True)]
    pallas_call x0 -> x1, Pallas kernels: none -> 147 us  [local(): pl.pallas_call(functools.partial(kernel, members, slots), out_shape=jax.S...]
    gather x5 -> x0, local copies, waits for them, and re-layouts: 35.9 us -> none  [the longest x2 15.5 us: arrange(): return jnp.take(blocks, picked, axis=0, mode='fill', fill_value=0)]
    dot_general x2 -> x0, matrix products: 21.7 us -> none  [the longest x1 12.6 us: local(): jnp.einsum('uab,ubc->uac', left_blocks, sources, preferred_element_type=j...]
    select_n x7 -> x0, other arithmetic: 16.4 us -> none  [the longest x2 11.8 us: arrange(): return jnp.take(blocks, picked, axis=0, mode='fill', fill_value=0)]
    all_to_all x2 -> x0, starting transfers between devices: 11.1 us -> none  [the longest x1 6.35 us: local(): lax.all_to_all(outgoing, 'sec', split_axis=0, concat_axis=0, tiled=True)]
    convert_element_type x1 -> x0, local copies, waits for them, and re-layouts: 8.62 us -> none  [local(): projected = jnp.einsum('uab,ubc->uac', left_blocks, sources, preferred_el...]
    ppermute x2 -> x0, starting transfers between devices: 6.46 us -> none  [the longest x1 4.54 us: padded_2(): lax.ppermute(lax.slice_in_dim(block, 0, width, axis=dim), axis, backward)]
  transfers between devices with their start and end apart: 4 -> 0, of which waited for: 2 -> 0; matrix products, arithmetic and copies ran while one was open for 1% -> 0% of each run, Pallas kernels for 0% -> 0%
where the time goes in v1:
time: 152 us
  Pallas kernels  147 us (97%)
  local copies, waits for them, and re-layouts  3.62 us (2%)
  other arithmetic  1.69 us (1%)
    pallas_call x1, Pallas kernels, local(): pl.pallas_call(functools.partial(kernel, members, slots), out_shape=jax.S...  147 us
    unnamed x9, local copies, waits for them, and re-layouts  3.62 us

profile of v1, /device:TPU:18, one launch (start us, length us, event | category | flops | bytes accessed | tf_op | source)
XLA Modules:
  0.0 152.2 jit_solution(18036558299881120119)
XLA Ops:
  0.0 0.9 convert_reduce_fusion
  0.9 0.7 iota_add_fusion
  1.6 0.1 select_reduce_fusion
  1.7 0.0 copy-start
  1.7 0.9 copy-done
  2.7 0.0 copy-start.1
  2.7 0.7 copy-done.1
  3.3 0.0 copy-start.2
  3.3 0.7 copy-done.2
  4.0 0.0 copy-start.3
  4.0 0.7 copy-done.3
  4.6 146.9 %route_and_multiply.1 = bf16[2,256,256]{2,1,0:T(8,128)(2,1)S(1)} custom-call(s32[48]{0:T(128)S(1)} %broadcast_add_fusion.picked_ref, s32[24]{0:T(128)S(1)} %copy-done.1, s32[2]{0:T(128)S(1)} %copy-done.2, s32[2]{0:T(128)S(1)} %copy-done.3, bf16[2,256,256]{2,1,0:T(8,128)(2,1)S(1)} %copy-done, bf16[48,256,256]{2,1,0:T(8,128)(2,1)} %bitcast.1, ...), custom_call_target="tpu_custom_call" | custom-call | tf_op jit(solution)/shard_map/route_and_multiply/pallas_call | solution.py:200
  151.5 0.7 copy.9
  (1 shorter events, 0.0 us)
Async XLA Ops:
  1.7 1.0 copy-start
  2.7 0.7 copy-start.1
  3.3 0.7 copy-start.2
  4.0 0.7 copy-start.3

commit v2 on v1

v2 whole, which is shorter than its diff:
```python
import functools

import jax
import jax.numpy as jnp
from jax import lax
from jax.experimental import pallas as pl
from jax.experimental.pallas import tpu as pltpu
from jax.sharding import PartitionSpec as P


def live_region(rows, columns, states):
    row = lax.broadcasted_iota(jnp.int32, (states, states), 0)
    column = lax.broadcasted_iota(jnp.int32, (states, states), 1)
    return (row < rows) & (column < columns)


def kernel(
    members,
    slots,
    numbers,
    two_site_hbm,
    left_env_hbm,
    right_env_hbm,
    out_ref,
    two_site,
    left_env,
    right_env,
    outgoing,
    incoming,
    projected,
    padded,
    total,
    load_sem,
    edge_send_sem,
    edge_recv_sem,
    send_sem,
    recv_sem,
):
    own = lax.axis_index("sec")
    sec_local, states = two_site.shape[0], two_site.shape[1]
    unit_count = left_env.shape[0]
    term_count = unit_count // sec_local
    half = members // 2
    own_half, own_place = own // half, own % half

    shift_start = members * slots
    left_start = shift_start + term_count
    right_start = left_start + sec_local

    two_site_copy = pltpu.make_async_copy(two_site_hbm, two_site, load_sem.at[0])
    right_copy = pltpu.make_async_copy(right_env_hbm, right_env, load_sem.at[1])
    left_copy = pltpu.make_async_copy(left_env_hbm, left_env, load_sem.at[2])
    two_site_copy.start()
    right_copy.start()

    barrier = pltpu.get_barrier_semaphore()

    def greet(step, carry):
        pl.semaphore_signal(barrier, inc=1, device_id={"sec": lax.rem(own + step, members)})
        return carry

    lax.fori_loop(1, members, greet, 0)

    two_site_copy.wait()
    for sector in range(sec_local):
        live = live_region(numbers[left_start + sector], numbers[right_start + sector], states)
        block = two_site[sector]
        padded[1 + sector] = jnp.where(live, block, jnp.zeros_like(block))

    pl.semaphore_wait(barrier, members - 1)

    def edge_copy(source, target, index, peer):
        return pltpu.make_async_remote_copy(
            src_ref=padded.at[source],
            dst_ref=padded.at[target],
            send_sem=edge_send_sem.at[index],
            recv_sem=edge_recv_sem.at[index],
            device_id={"sec": peer},
        )

    up = edge_copy(sec_local, 0, 0, lax.rem(own + 1, members))
    down = edge_copy(1, sec_local + 1, 1, lax.rem(own + members - 1, members))
    has_up, has_down = own < members - 1, own > 0

    pl.when(has_up)(up.start)
    pl.when(has_down)(down.start)

    def partner(step, sign):
        across = step < half
        move = jnp.where(across, step, step - half + 1)
        base = jnp.where(across, 1 - own_half, own_half) * half
        return base + lax.rem(own_place + sign * move + half, half)

    def block_copy(step):
        return pltpu.make_async_remote_copy(
            src_ref=outgoing.at[pl.ds(step * slots, slots)],
            dst_ref=incoming.at[pl.ds(step * slots, slots)],
            send_sem=send_sem.at[step],
            recv_sem=recv_sem.at[step],
            device_id={"sec": partner(step, 1)},
        )

    right_copy.wait()
    left_copy.start()

    def send(step, carry):
        offset = lax.rem(own - partner(step, 1) + members, members)
        for slot in range(slots):
            unit = jnp.minimum(numbers[offset * slots + slot], unit_count - 1)
            outgoing[step * slots + slot] = right_env[unit]
        block_copy(step).start()
        return carry

    lax.fori_loop(0, members - 1, send, 0)
    for slot in range(slots):
        unit = jnp.minimum(numbers[slot], unit_count - 1)
        incoming[(members - 1) * slots + slot] = right_env[unit]

    @pl.when(own == 0)
    def _():
        padded[0] = jnp.zeros(padded.shape[1:], padded.dtype)

    @pl.when(own == members - 1)
    def _():
        padded[sec_local + 1] = jnp.zeros(padded.shape[1:], padded.dtype)

    pl.when(has_up)(up.wait_send)
    pl.when(has_down)(down.wait_send)
    pl.when(has_down)(up.wait_recv)
    pl.when(has_up)(down.wait_recv)
    left_copy.wait()

    def project(unit, carry):
        source = padded[unit // term_count + 1 - numbers[shift_start + unit % term_count]]
        projected[unit] = jnp.dot(
            left_env[unit], source, preferred_element_type=jnp.float32
        ).astype(jnp.bfloat16)
        return carry

    lax.fori_loop(0, unit_count, project, 0)

    total[...] = jnp.zeros_like(total)

    def multiply(step, offset):
        units = [numbers[offset * slots + slot] for slot in range(slots)]
        factors = [projected[jnp.minimum(unit, unit_count - 1)] for unit in units]
        rights = jnp.concatenate([incoming[step * slots + slot] for slot in range(slots)], axis=1)
        for sector in range(sec_local):
            lefts = jnp.concatenate(
                [
                    jnp.where(unit // term_count == sector, factor, jnp.zeros_like(factor))
                    for unit, factor in zip(units, factors)
                ],
                axis=1,
            )
            total[sector] += lax.dot_general(
                lefts, rights, (((1,), (1,)), ((), ())), preferred_element_type=jnp.float32
            )

    multiply(members - 1, 0)

    def arrive(step, carry):
        turn = lax.rem(step + half, members - 1)
        offset = lax.rem(partner(turn, -1) - own + members, members)
        block_copy(turn).wait_recv()
        multiply(turn, offset)
        return carry

    lax.fori_loop(0, members - 1, arrive, 0)

    def sent(step, carry):
        block_copy(step).wait_send()
        return carry

    lax.fori_loop(0, members - 1, sent, 0)

    for sector in range(sec_local):
        live = live_region(numbers[left_start + sector], numbers[right_start + sector], states)
        value = total[sector]
        out_ref[sector] = jnp.where(live, value, jnp.zeros_like(value)).astype(out_ref.dtype)


def local(two_site, left_size, right_size, term_shift, route_offset, left_env, right_env):
    members = lax.axis_size("sec")
    sec_local, states = two_site.shape[0], two_site.shape[1]
    unit_count = right_env.shape[0]
    slots = (unit_count + members - 1) // members
    slot_total = members * slots
    unit_index = jnp.arange(unit_count, dtype=jnp.int32)
    same_offset = route_offset[None, :] == route_offset[:, None]
    earlier = unit_index[None, :] < unit_index[:, None]
    unit_rank = jnp.sum((same_offset & earlier).astype(jnp.int32), axis=1)
    place = route_offset * slots + unit_rank
    slot_index = jnp.arange(slot_total, dtype=jnp.int32)
    picked = unit_count + jnp.sum(
        jnp.where(place[None, :] == slot_index[:, None], unit_index[None, :] - unit_count, 0),
        axis=1,
    )
    numbers = jnp.concatenate([picked, term_shift, left_size, right_size])
    block = (states, states)
    hbm = pl.BlockSpec(memory_space=pl.ANY)
    return pl.pallas_call(
        functools.partial(kernel, members, slots),
        out_shape=jax.ShapeDtypeStruct(two_site.shape, two_site.dtype),
        in_specs=[pl.BlockSpec(memory_space=pltpu.SMEM), hbm, hbm, hbm],
        out_specs=pl.BlockSpec(memory_space=pltpu.VMEM),
        scratch_shapes=[
            pltpu.VMEM(two_site.shape, jnp.bfloat16),
            pltpu.VMEM((unit_count,) + block, jnp.bfloat16),
            pltpu.VMEM((unit_count,) + block, jnp.bfloat16),
            pltpu.VMEM((slot_total,) + block, jnp.bfloat16),
            pltpu.VMEM((slot_total,) + block, jnp.bfloat16),
            pltpu.VMEM((unit_count,) + block, jnp.bfloat16),
            pltpu.VMEM((sec_local + 2,) + block, jnp.bfloat16),
            pltpu.VMEM((sec_local,) + block, jnp.float32),
            pltpu.SemaphoreType.DMA((3,)),
            pltpu.SemaphoreType.DMA((2,)),
            pltpu.SemaphoreType.DMA((2,)),
            pltpu.SemaphoreType.DMA((members - 1,)),
            pltpu.SemaphoreType.DMA((members - 1,)),
        ],
        compiler_params=pltpu.CompilerParams(
            collective_id=0, has_side_effects=True, vmem_limit_bytes=50 * 1024 * 1024
        ),
        name="route_and_multiply",
    )(numbers, two_site, left_env.reshape((unit_count,) + block), right_env)


def solution(mesh):
    in_specs = (
        P(("groups", "sec"), None, None),
        P(("groups", "sec")),
        P(("groups", "sec")),
        P("groups"),
        P("groups"),
        P(("groups", "sec"), None, None, None),
        P(("groups", "sec"), None, None),
    )
    out_specs = P(("groups", "sec"), None, None)
    return jax.shard_map(local, mesh=mesh, in_specs=in_specs, out_specs=out_specs, check_vma=False)
```

time: 152 us -> 154 us (1.013)
  the two profiles are of different devices: /device:TPU:18 before, /device:TPU:1 now
where the time goes in v2:
time: 154 us
  Pallas kernels  150 us (97%)
  other arithmetic  2.46 us (2%)
  local copies, waits for them, and re-layouts  1.66 us (1%)
    pallas_call x1, Pallas kernels, local(): pl.pallas_call(functools.partial(kernel, members, slots), out_shape=jax.S...  150 us

profile of v2, /device:TPU:1, one launch (start us, length us, event | category | flops | bytes accessed | tf_op | source)
XLA Modules:
  0.0 153.9 jit_solution(13623997861207395296)
XLA Ops:
  0.0 0.9 convert_reduce_fusion
  0.9 0.7 iota_add_fusion
  1.6 0.1 select_reduce_fusion
  1.7 0.8 pad_add_fusion.numbers
  2.5 0.0 copy-start
  2.5 0.9 copy-done
  3.4 149.7 %route_and_multiply.1 = bf16[2,256,256]{2,1,0:T(8,128)(2,1)S(1)} custom-call(s32[76]{0:T(128)S(1)} %pad_add_fusion.numbers, bf16[2,256,256]{2,1,0:T(8,128)(2,1)S(1)} %copy-done, bf16[48,256,256]{2,1,0:T(8,128)(2,1)} %bitcast.1, bf16[48,256,256]{2,1,0:T(8,128)(2,1)} %right_env_hbm.1), custom_call_target="tpu_custom_call" | custom-call | tf_op jit(solution)/shard_map/route_and_multiply/pallas_call | solution.py:202
  153.2 0.7 copy.9
  (1 shorter events, 0.0 us)
Async XLA Ops:
  2.5 1.0 copy-start

commit v3 on v2

--- a/solution.py
+++ b/solution.py
@@ -40,8 +40,8 @@
     sec_local, states = two_site.shape[0], two_site.shape[1]
     unit_count = left_env.shape[0]
     term_count = unit_count // sec_local
-    half = members // 2
-    own_half, own_place = own // half, own % half
+    quarter = members // 4
+    own_quarter, own_place = own // quarter, own % quarter
 
     shift_start = members * slots
     left_start = shift_start + term_count
@@ -86,10 +86,17 @@
     pl.when(has_down)(down.start)
 
     def partner(step, sign):
-        across = step < half
-        move = jnp.where(across, step, step - half + 1)
-        base = jnp.where(across, 1 - own_half, own_half) * half
-        return base + lax.rem(own_place + sign * move + half, half)
+        group = step // quarter
+        move = jnp.where(group < 3, step % quarter, step - 3 * quarter + 1)
+        ahead, back = (2 * own_quarter + 1) % 5, (3 * own_quarter + 2) % 5
+        if sign < 0:
+            ahead, back = back, ahead
+        other = jnp.where(
+            group == 0,
+            ahead,
+            jnp.where(group == 1, 3 - own_quarter, jnp.where(group == 2, back, own_quarter)),
+        )
+        return other * quarter + lax.rem(own_place + sign * move + quarter, quarter)
 
     def block_copy(step):
         return pltpu.make_async_remote_copy(
@@ -160,7 +167,7 @@
     multiply(members - 1, 0)
 
     def arrive(step, carry):
-        turn = lax.rem(step + half, members - 1)
+        turn = lax.rem(step + 3 * quarter, members - 1)
         offset = lax.rem(partner(turn, -1) - own + members, members)
         block_copy(turn).wait_recv()
         multiply(turn, offset)

time: 154 us -> 149 us (0.968)
  the two profiles are of different devices: /device:TPU:1 before, /device:TPU:18 now
where the time goes in v3:
time: 149 us; the launch traced here: 147 us
  Pallas kernels  143 us (96%)
  other arithmetic  2.46 us (2%)
  local copies, waits for them, and re-layouts  1.66 us (1%)
    pallas_call x1, Pallas kernels, local(): pl.pallas_call(functools.partial(kernel, members, slots), out_shape=jax.S...  143 us

profile of v3, /device:TPU:18, one launch (start us, length us, event | category | flops | bytes accessed | tf_op | source)
XLA Modules:
  0.0 146.8 jit_solution(13703258369830648484)
XLA Ops:
  0.0 0.9 convert_reduce_fusion
  0.9 0.7 iota_add_fusion
  1.6 0.1 select_reduce_fusion
  1.7 0.8 pad_add_fusion.numbers
  2.5 0.0 copy-start
  2.5 0.9 copy-done
  3.4 142.7 %route_and_multiply.1 = bf16[2,256,256]{2,1,0:T(8,128)(2,1)S(1)} custom-call(s32[76]{0:T(128)S(1)} %pad_add_fusion.numbers, bf16[2,256,256]{2,1,0:T(8,128)(2,1)S(1)} %copy-done, bf16[48,256,256]{2,1,0:T(8,128)(2,1)} %bitcast.1, bf16[48,256,256]{2,1,0:T(8,128)(2,1)} %right_env_hbm.1), custom_call_target="tpu_custom_call" | custom-call | tf_op jit(solution)/shard_map/route_and_multiply/pallas_call | solution.py:209
  146.1 0.7 copy.9
  (1 shorter events, 0.0 us)
Async XLA Ops:
  2.5 1.0 copy-start
